TPU v7x, 32 devices: a whole 2x2x4 slice. The times are simulated.
32 devices in a mesh: dp: 8 (over y, x, core), tensor: 4 (over z).
Axes of the slice: x: 2, y: 2, z: 4, core: 2. Of those that a mesh axis runs over, the one named last changes fastest.
Arguments:
- hidden: bfloat16 [16384, 768], P(('dp', 'tensor')), may hold values from -6 to 6
- page_boxes: int32 [16384, 4], P(('dp', 'tensor')), may hold values from 0 to 1000
- lengths: int32 [32], P('dp'), may hold values from 128 to 512
- table_x: bfloat16 [1024, 768], replicated, may hold values from -3 to 3
- table_y: bfloat16 [1024, 768], replicated, may hold values from -3 to 3
- in_weight: bfloat16 [3, 768, 768], P(None, None, 'tensor'), may hold values from -0.21875 to 0.21875
- in_bias: float32 [2, 768], P(None, 'tensor'), may hold values from -0.6 to 0.6
- out_weight: bfloat16 [768, 768], P('tensor'), may hold values from -1.25 to 1.25
- out_bias: float32 [768], replicated, may hold values from -1.5 to 1.5
- up_weight: bfloat16 [768, 3072], P(None, 'tensor'), may hold values from -0.21875 to 0.21875
- up_bias: float32 [3072], P('tensor'), may hold values from -1.5 to 1.5
- down_weight: bfloat16 [3072, 768], P('tensor'), may hold values from -0.109375 to 0.109375
- down_bias: float32 [768], replicated, may hold values from -1.5 to 1.5
- norm_gain: float32 [2, 768], replicated, may hold values from 0.25 to 1.75
- norm_bias: float32 [2, 768], replicated, may hold values from -1.5 to 1.5
- cotangent: bfloat16 [16384, 768], P(('dp', 'tensor')), may hold values from -6 to 6
Outputs:
- layer_out: bfloat16 [16384, 768], P(('dp', 'tensor'))
- grad_hidden: float32 [16384, 768], P(('dp', 'tensor'))
- grad_table_x: float32 [1024, 768], replicated
- grad_table_y: float32 [1024, 768], replicated
- grad_in_weight: float32 [3, 768, 768], P(None, None, 'tensor')
- grad_in_bias: float32 [2, 768], P(None, 'tensor')
- grad_out_weight: float32 [768, 768], P('tensor')
- grad_out_bias: float32 [768], replicated
- grad_up_weight: float32 [768, 3072], P(None, 'tensor')
- grad_up_bias: float32 [3072], P('tensor')
- grad_down_weight: float32 [3072, 768], P('tensor')
- grad_down_bias: float32 [768], replicated
- grad_norm_gain: float32 [2, 768], replicated
- grad_norm_bias: float32 [2, 768], replicated
All inputs are finite; a program needn't handle non-finite values.
Results may differ from a plain program's by a relative error of at most 0.02.
The roundings to bfloat16 on the way count: a program that leaves them out, or rounds other values in their place, can miss the bound.
Values may be sent and summed in bfloat16 or wider, within the bound.
A program may use at most 128 MiB of HBM per device.

v0:
```python
from functools import partial

import jax
import jax.numpy as jnp
from jax import lax
from jax.experimental import pallas as pl
from jax.experimental.pallas import tpu as pltpu
from jax.sharding import PartitionSpec as P

HEAD = 64
EPS = 1e-12
MESH = pl.DeviceIdType.MESH
f32 = jnp.float32
bf16 = jnp.bfloat16

R = 48
RT = 16
FR = 16
XR = R - FR
ZR = 16


def dot(a, b, ca, cb):
    return lax.dot_general(a, b, (((ca,), (cb,)), ((), ())), preferred_element_type=f32)


def kernel(
    dp,
    hidden,
    boxes,
    lengths,
    tables_x,
    tables_y,
    in_w,
    in_b,
    out_w,
    out_b,
    up_w,
    up_b,
    down_w,
    down_b,
    gain,
    nbias,
    cotangent,
    layer_out,
    grad_hidden,
    G,
    GT,
    W,
    G2,
    pre,
    act,
    gp,
    qkv,
    ctx,
    lse,
    resb,
    midb,
    bgrad,
    hid,
    res,
    total,
    n1,
    r1,
    bias,
    vec,
    core_land,
    core_land_t,
    lands0,
    lands1,
    lands2,
    lands_t,
    lands_f,
    lands_ft,
    zl0,
    zl1,
    zl2,
    zlt,
    zlf,
    zlft,
    extra,
    extra_t,
    loc,
    bs,
    br,
    gzs,
    gzr,
    gds,
    gdr,
    xs,
    xr,
    cs,
    cr,
    ks,
    kr,
    credit,
    rs,
    rr,
    zs,
    zr,
    es,
    er,
):
    d = lax.axis_index("dp")
    t = lax.axis_index("tensor")
    c = d % 2
    x = (d // 2) % 2
    y = (d // 4) % 2
    X = (d + 2 - 4 * x, t)
    Y = (d + 4 - 8 * y, t)
    C = (d + 1 - 2 * c, t)
    extras = []
    step = 8
    while step < dp:
        extras.append((d + step - 2 * step * ((d // step) % 2), t))
        step *= 2

    def remote(src, dst, send, recv, dev):
        return pltpu.make_async_remote_copy(
            src_ref=src, dst_ref=dst, send_sem=send, recv_sem=recv, device_id=dev, device_id_type=MESH
        )

    def wait_recv(ref, sem):
        remote(ref, ref, sem, sem, C).wait_recv()

    def wait_send(ref, sem):
        remote(ref, ref, sem, sem, C).wait_send()

    barrier = pltpu.get_barrier_semaphore()
    zpeers = [(d, (t + j) % 4) for j in range(1, 4)]
    peers = [X, Y, C] + zpeers + extras
    for peer in peers:
        pl.semaphore_signal(barrier, inc=1, device_id=peer, device_id_type=MESH)

    local = [
        pltpu.make_async_copy(in_w.at[pl.ds(0, 2)], W.at[0, t, 0], loc.at[0]),
        pltpu.make_async_copy(tables_x, pre.at[pl.ds(0, 1024)], loc.at[1]),
        pltpu.make_async_copy(tables_y, pre.at[pl.ds(1024, 1024)], loc.at[2]),
        pltpu.make_async_copy(hidden, hid, loc.at[3]),
        pltpu.make_async_copy(out_w, W.at[0, t, 1, 1], loc.at[4]),
        pltpu.make_async_copy(up_w, W.at[1, t], loc.at[5]),
        pltpu.make_async_copy(down_w, W.at[2, t], loc.at[6]),
        pltpu.make_async_copy(in_w.at[2], W.at[0, t, 1, 0], loc.at[7]),
    ]
    for i in (0, 7, 4, 1, 2, 3, 5, 6):
        local[i].start()
    bias[t] = jnp.zeros((8, 768), f32)
    bias[t, 0:1, :] = up_b[...].reshape(1, 768)
    bias[t, 1:2, 0:192] = in_b[0:1, :]
    bias[t, 1:2, 384:576] = in_b[1:2, :]
    def entry_local():
        local[0].wait()
        local[4].wait()
        local[7].wait()

    def entry_barrier():
        pl.semaphore_wait(barrier, len(peers))

    entry_barrier()
    entry_local()

    half = t // 2
    near = t * (1 - half) + (3 - t) * half

    def other(j):
        base = j + 1 - near * ((3 - j) // 3)
        return base * (1 - half) + (3 - base) * half

    def z_own(src, dst, ss, rsem):
        @pl.when(t > 0)
        def _():
            remote(src, dst, ss(0), rsem, (d, t - 1)).start()

        @pl.when(t < 3)
        def _():
            remote(src, dst, ss(1), rsem, (d, t + 1)).start()

    def z_arrive(ref, tp, send, recv):
        wait_recv(ref, recv)

        @pl.when(jnp.logical_and(tp < t, t < 3))
        def _():
            remote(ref, ref, send, recv, (d, t + 1)).start()

        @pl.when(jnp.logical_and(tp > t, t > 0))
        def _():
            remote(ref, ref, send, recv, (d, t - 1)).start()

    def z_drain(ref, ss):
        @pl.when(t > 0)
        def _():
            wait_send(ref, ss(0))

        @pl.when(t < 3)
        def _():
            wait_send(ref, ss(1))

    def z_arrive_drain(ref, tp, send):
        @pl.when(jnp.logical_or(jnp.logical_and(tp < t, t < 3), jnp.logical_and(tp > t, t > 0)))
        def _():
            wait_send(ref, send)

    def xy_own(src, dst, i):
        a, b = src.at[0], src.at[1]
        da, db = dst.at[c, y, x, 0], dst.at[c, y, x, 1]
        remote(a, da, xs.at[i, 0], xr.at[i, 0], X).start()
        remote(b, db, xs.at[i, 2], xr.at[i, 2], Y).start()
        remote(a, da, xs.at[i, 1], xr.at[i, 1], Y).start()
        remote(b, db, xs.at[i, 3], xr.at[i, 3], X).start()

    def xy_relay(ref, i, ra=slice(None), rb=slice(None)):
        a, b = ref.at[c, y, 1 - x, 0, ra], ref.at[c, 1 - y, x, 1, rb]
        wait_recv(a, xr.at[i, 0])
        remote(a, a, xs.at[i, 4], xr.at[i, 4], Y).start()
        wait_recv(b, xr.at[i, 2])
        remote(b, b, xs.at[i, 5], xr.at[i, 5], X).start()

    def xy_finish(ref, i, ra=slice(None), rb=slice(None)):
        wait_recv(ref.at[c, 1 - y, x, 0, ra], xr.at[i, 1])
        wait_recv(ref.at[c, y, 1 - x, 1, rb], xr.at[i, 3])
        wait_recv(ref.at[c, 1 - y, 1 - x, 0, ra], xr.at[i, 4])
        wait_recv(ref.at[c, 1 - y, 1 - x, 1, rb], xr.at[i, 5])
        remote(ref.at[c], ref.at[c], cs.at[i], cr.at[i], C).start()

    def xy_done(ref, i):
        wait_recv(ref.at[1 - c], cr.at[i])

    def xy_drain(ref, i, ra=slice(None), rb=slice(None)):
        for k in range(6):
            wait_send(ref.at[c, 0, 0, 0, ra if k in (0, 1, 4) else rb], xs.at[i, k])
        wait_send(ref.at[c], cs.at[i])

    def rows_of(b, h):
        return pl.ds(0, R - ZR) if b + h == 2 else pl.ds(0, R)

    def both(b):
        return rows_of(b, 0), rows_of(b, 1)

    def whole(b, tp):
        return W.at[b, tp, c, :, :, 2 - b, pl.ds(R - ZR, ZR)]

    def whole_own(b):
        z_own(whole(b, t), whole(b, t), lambda k: gds.at[b - 1, k], gdr.at[b - 1, t])

    def whole_in(i):
        b, j = i // 3, i % 3
        z_arrive(whole(b, other(j)), other(j), gds.at[b - 1, 2 + j], gdr.at[b - 1, other(j)])

    def gz_own(b):
        for h in range(2):
            ref = W.at[b, t, c, y, x, h, rows_of(b, h)]
            z_own(ref, ref, lambda k: gzs.at[b, k, h], gzr.at[b, t, h])

    def gz_end(b):
        @pl.when(jnp.logical_or(t == 0, t == 3))
        def _():
            gz_own(b)

    def gz_middle(b):
        @pl.when(jnp.logical_and(t > 0, t < 3))
        def _():
            gz_own(b)

    def e1(i):
        b, j = i // 3, i % 3
        tp = other(j)
        for h in range(2):
            ref = W.at[b, tp, c, y, x, h, rows_of(b, h)]
            z_arrive(ref, tp, gzs.at[b, 2 + j, h], gzr.at[b, tp, h])
            for dev, k in ((X, 0), (Y, 1)) if h == 0 else ((Y, 2), (X, 3)):
                remote(ref, ref, xs.at[i, k], xr.at[i, k], dev).start()

    def e2(i):
        xy_relay(W.at[i // 3, other(i % 3)], i, *both(i // 3))

    def e3(i):
        xy_finish(W.at[i // 3, other(i % 3)], i, *both(i // 3))

    def e4(i):
        xy_done(W.at[i // 3, other(i % 3)], i)

    gz_own(0)
    for j in range(3):
        remote(bias.at[t], bias.at[t], bs.at[j], br.at[2 - j], zpeers[j]).start()

    def one_hot(first, second, levels):
        return ((first == levels).astype(f32) + (second == levels).astype(f32)).astype(bf16)

    levels = lax.broadcasted_iota(jnp.int32, (1024, 1), 0)

    def embed():
        for i in (1, 2, 3):
            local[i].wait()
        horizontal = one_hot(boxes[0:1], boxes[2:3], levels)
        vertical = one_hot(boxes[1:2], boxes[3:4], levels)
        residual = (
            hid[...].astype(f32)
            + dot(horizontal, pre[0:1024, :], 0, 0)
            + dot(vertical, pre[1024:2048, :], 0, 0)
        )
        res[...] = residual
        resb[...] = residual.astype(bf16)
        total[...] = jnp.zeros_like(total)

    embed()
    local[5].wait()
    local[6].wait()
    cot_copy = pltpu.make_async_copy(cotangent, hid, loc.at[3])
    cot_copy.start()

    def biases():
        for j in range(3):
            tz = (t + 3 - j) % 4
            wait_recv(bias.at[tz], br.at[2 - j])

    length = lengths[t]
    visible = lax.broadcasted_iota(jnp.int32, (512, 1), 0) < length
    scaling = HEAD**-0.5

    def project(tp):
        weight = W[0, tp].reshape(768, 768)
        qkv[tp] = (dot(resb[...], weight[0:576], 1, 1) + bias[tp, 1:2, 0:576]).astype(bf16)

    def heads(tp):
        for j in range(3):
            q = qkv[tp, :, j * 64 : (j + 1) * 64]
            k = qkv[tp, :, 192 + j * 64 : 192 + (j + 1) * 64]
            v = qkv[tp, :, 384 + j * 64 : 384 + (j + 1) * 64]
            scores = jnp.where(visible, dot(k, q, 1, 1) * scaling, -1e30)
            top = jnp.max(scores, axis=0, keepdims=True)
            exponent = jnp.exp(scores - top)
            sums = jnp.sum(exponent, axis=0, keepdims=True)
            attend = (exponent * (1.0 / sums)).astype(bf16)
            ctx[tp, :, j * 64 : (j + 1) * 64] = dot(attend, v, 0, 0).astype(bf16)
            lse[tp, j : j + 1, :] = top + jnp.log(sums)
        total[...] += dot(ctx[tp], W[0, tp, 1, 1].reshape(192, 768), 1, 0)

    def up(tp):
        hidden_pre = dot(midb[...], W[1, tp].reshape(768, 768), 1, 0) + bias[tp, 0:1, :]
        cdf = 0.5 * (1.0 + lax.erf(hidden_pre * 0.7071067811865476))
        act[pl.ds(2 * tp, 2)] = (hidden_pre * cdf).astype(bf16).reshape(2, 2, 2, 2, 2, RT, 768)
        slope = cdf + hidden_pre * jnp.exp(-0.5 * hidden_pre * hidden_pre) * 0.3989422804014327
        gp[tp] = slope.astype(bf16)

    def down(tp):
        total[...] += dot(act[pl.ds(2 * tp, 2)].reshape(512, 768), W[2, tp].reshape(768, 768), 1, 0)

    def normalize(value):
        average = jnp.mean(value, axis=-1, keepdims=True)
        centered = value - average
        inverse = lax.rsqrt(jnp.mean(centered * centered, axis=-1, keepdims=True) + EPS)
        return centered * inverse, inverse

    def normalize_back(gradient, normed, inverse, gain_row):
        scaled = gradient * gain_row
        inner = (
            scaled
            - jnp.mean(scaled, axis=-1, keepdims=True)
            - normed * jnp.mean(scaled * normed, axis=-1, keepdims=True)
        )
        return inverse * inner

    def row_sum(value):
        return jnp.sum(value, axis=0, keepdims=True)

    def out_norm():
        normed, inverse = normalize(res[...] + total[...] + out_b[...].reshape(1, 768))
        n1[...] = normed
        r1[...] = inverse
        middle = normed * gain[0:1] + nbias[0:1]
        res[...] = middle
        midb[...] = middle.astype(bf16)
        total[...] = jnp.zeros_like(total)

    def drain_items(b):
        def one(j, _):
            xy_drain(W.at[0, 0], 3 * b + j, *both(b))
            return 0

        lax.fori_loop(0, 3, one, 0)

    def drain_z(b):
        for h in range(2):
            ref = W.at[0, 0, 0, 0, 0, 0, rows_of(b, h)]
            z_drain(ref, lambda k: gzs.at[b, k, h])
            for j in range(3):
                z_arrive_drain(ref, other(j), gzs.at[b, 2 + j, h])

    def drain_whole(b):
        z_drain(whole(b, 0), lambda k: gds.at[b - 1, k])
        for j in range(3):
            z_arrive_drain(whole(b, 0), other(j), gds.at[b - 1, 2 + j])

    def events(k, *turns):
        for turn, calls in enumerate(turns):
            if calls:

                @pl.when(k == turn)
                def _(calls=calls):
                    for call, *given in calls:
                        call(*given)

    def quarter(k):
        own = (3 - k) // 3
        return own * t + (1 - own) * other(k - 1)

    e1(0)
    e1(1)
    gz_end(1)
    e2(0)
    e1(2)
    gz_middle(1)
    e2(1)
    biases()

    def attend(k, _):
        tp = quarter(k)
        project(tp)
        events(
            k,
            [(e2, 2)],
            [(e1, 4), (whole_own, 1), (gz_end, 2), (e3, 1)],
            [(e3, 2)],
            [(e1, 7), (e2, 5), (whole_in, 3)],
        )
        heads(tp)
        events(
            k,
            [(e3, 0), (e1, 3), (e4, 0)],
            [(e1, 5), (gz_middle, 2), (e2, 3), (e4, 1)],
            [(e2, 4), (e1, 6), (e4, 2)],
            [(e1, 8), (whole_own, 2), (e3, 3)],
        )
        return 0

    def widen(k, _):
        up(quarter(k))
        events(
            k,
            [(e4, 3), (whole_in, 4), (e3, 4)],
            [(e2, 7), (whole_in, 5), (e3, 5), (e4, 4), (whole_in, 6)],
            [(e2, 8), (whole_in, 7), (e3, 6), (e4, 5)],
        )
        return 0

    def drain_early():
        drain_items(0)
        drain_items(1)
        for b in range(3):
            drain_z(b)
        drain_whole(1)

    def drain_late():
        drain_items(2)
        drain_whole(2)

    def narrow(k, _):
        down(quarter(k))
        events(k, [(e3, 7), (whole_in, 8), (drain_early,), (e4, 6)], [(e3, 8), (e4, 7)], [(e4, 8)])
        return 0

    lax.fori_loop(0, 4, attend, 0)
    out_norm()
    e2(6)
    lax.fori_loop(0, 4, widen, 0)
    lax.fori_loop(0, 4, narrow, 0)

    normed, inverse = normalize(res[...] + total[...] + down_b[...].reshape(1, 768))
    pre[1536:2048, :] = (normed * gain[1:2] + nbias[1:2]).astype(bf16)
    out_copy = pltpu.make_async_copy(pre.at[pl.ds(1536, 512)], layer_out, loc.at[8])
    out_copy.start()
    cot_copy.wait()
    gradient = hid[...].astype(f32)
    final_grad = normalize_back(gradient, normed, inverse, gain[1:2])
    res[...] = final_grad
    bgrad[...] = final_grad.astype(bf16)
    vec[...] = jnp.zeros_like(vec)
    vec[1:2, :] = row_sum(bgrad[...].astype(f32))
    vec[3:4, :] = row_sum(gradient * normed)
    vec[5:6, :] = row_sum(gradient)

    def core_send(ref, n, tp):
        remote(ref.at[tp, 1 - c], core_land.at[n % 6], ks.at[n], kr.at[n], C).start()

    def core_add(ref, n, tp):
        wait_recv(core_land.at[n % 6], kr.at[n])
        ref[tp, c] = ref[tp, c] + core_land[n % 6]

    def free():
        pl.semaphore_signal(credit, inc=1, device_id=C, device_id_type=MESH)

    def wait_free():
        pl.semaphore_wait(credit, 1)

    def xy1_send(ref, part, rows, lands, lp, g):
        a = ref.at[part, c, :, 1 - x, 0, rows]
        b = ref.at[part, c, 1 - y, :, 1, rows]
        remote(a, lands[0].at[lp], rs.at[g, 0], rr.at[g, 0], X).start()
        remote(b, lands[1].at[lp], rs.at[g, 1], rr.at[g, 1], Y).start()

    def xy1_add(ref, part, rows, lands, lp, g):
        wait_recv(lands[0].at[lp], rr.at[g, 0])
        ref[part, c, :, x, 0, rows] = ref[part, c, :, x, 0, rows] + lands[0][lp]
        remote(ref.at[part, c, 1 - y, x, 0, rows], lands[3].at[lp], rs.at[g, 3], rr.at[g, 3], Y).start()
        wait_recv(lands[1].at[lp], rr.at[g, 1])
        ref[part, c, y, :, 1, rows] = ref[part, c, y, :, 1, rows] + lands[1][lp]
        remote(ref.at[part, c, y, 1 - x, 1, rows], lands[2].at[lp], rs.at[g, 2], rr.at[g, 2], X).start()

    def xy2_add(ref, part, rows, lands, lp, g):
        wait_recv(lands[3].at[lp], rr.at[g, 3])
        ref[part, c, y, x, 0, rows] = ref[part, c, y, x, 0, rows] + lands[3][lp]
        wait_recv(lands[2].at[lp], rr.at[g, 2])
        ref[part, c, y, x, 1, rows] = ref[part, c, y, x, 1, rows] + lands[2][lp]

    def xy_rs_drain(lands, lp, g):
        for k in range(4):
            wait_send(lands[k].at[lp], rs.at[g, k])

    def z_send(ref, rows, land, g):
        for j in range(1, 4):
            k = (t + j) % 4
            remote(ref.at[k, c, y, x, :, rows], land.at[j - 1], zs.at[g, j - 1], zr.at[g, j - 1], (d, k)).start()

    def zk_send(ref, rows, land, g, k):
        @pl.when(t != k)
        def _():
            slot = (k - t + 3) % 4
            remote(ref.at[k, c, y, x, :, rows], land.at[slot], zs.at[g, slot], zr.at[g, slot], (d, k)).start()

    def z_sum(ref, rows, land, g):
        for j in range(3):
            wait_recv(land.at[j], zr.at[g, j])
        value = ref[t, c, y, x, :, rows].astype(f32)
        for j in range(3):
            value = value + land[j].astype(f32)
        ref[t, c, y, x, :, rows] = value.astype(bf16)

    def z_drain_sum(land, g):
        for j in range(3):
            wait_send(land.at[j], zs.at[g, j])

    def zf_send(ref, rows, land, g, k):
        @pl.when(t != k)
        def _():
            slot = (k - t + 3) % 4
            remote(ref.at[k, c, :, :, :, rows], land.at[slot], zs.at[g, slot], zr.at[g, slot], (d, k)).start()

    def zf_sum(ref, rows, land, g):
        for j in range(3):
            wait_recv(land.at[j], zr.at[g, j])
        value = ref[t, c, :, :, :, rows].astype(f32)
        for j in range(3):
            value = value + land[j].astype(f32)
        ref[t, c, :, :, :, rows] = value.astype(bf16)

    def across(ref, land, g):
        for i, peer in enumerate(extras):
            copy = remote(ref, land.at[i], es.at[g, i], er.at[g, i], peer)
            copy.start()
            copy.wait()
            ref[...] = ref[...] + land[i]

    g1 = W.at[2]
    g0 = W.at[1]
    low, high, every = pl.ds(0, 2), pl.ds(2, 2), pl.ds(0, 4)
    rows_x, rows_f, rows, rows_t = pl.ds(0, XR), pl.ds(XR, FR), pl.ds(0, R), pl.ds(0, RT)
    tables = [act.at[pl.ds(0, 4)], act.at[pl.ds(4, 4)]]
    b2_low, b2_high = (G2, low, rows_x, lands2, low, 0), (G2, high, rows_x, lands2, high, 1)
    b1_low, b1_high = (g1, low, rows, lands1, low, 2), (g1, high, rows, lands1, high, 3)
    b0_low = (g0, low, rows, lands0, low, 4)
    b0_q2, b0_q3 = (g0, pl.ds(2, 1), rows, lands0, pl.ds(2, 1), 5), (g0, pl.ds(3, 1), rows, lands0, pl.ds(3, 1), 6)
    table1 = (tables[1], every, rows_t, lands_t, every, 8)
    f2, ft = (G2, t, rows_f, lands_f, 0, 9), (tables[0], t, rows_t, lands_ft, 0, 7)
    z0, z1, z2 = (g0, rows, zl0, 0), (g1, rows, zl1, 1), (G2, rows_x, zl2, 2)
    zt1 = (tables[1], rows_t, zlt, 4)
    zf2, zft = (G2, rows_f, zlf, 7), (tables[0], rows_t, zlft, 3)

    def span(i):
        return pl.ds(pl.multiple_of(i * 512, 512), 512)

    def down_grad(i):
        activated = act[pl.ds(2 * i, 2)].reshape(512, 768)
        G2[i] = dot(activated, bgrad[...], 0, 0).astype(bf16).reshape(2, 2, 2, 2, R, 768)
        core_send(G2, i, i)

    def down_act(i):
        grad = dot(bgrad[...], W[2, i].reshape(768, 768), 1, 1).astype(bf16)
        pre_grad = (grad.astype(f32) * gp[i].astype(f32)).astype(bf16)
        pre[span(i), :] = pre_grad
        vec[pl.ds(6 + i, 1), :] = row_sum(pre_grad.astype(f32))

    def down_add(i):
        core_add(G2, i, i)
        free()
        zf_send(*zf2, i)

    def up_grad(i):
        g1[i] = dot(midb[...], pre[span(i), :], 0, 0).astype(bf16).reshape(2, 2, 2, 2, R, 768)

        @pl.when(i >= 2)
        def _():
            wait_free()

        core_send(g1, 4 + i, i)

    def up_act(i):
        res[...] += dot(pre[span(i), :], W[1, i].reshape(768, 768), 1, 1)

    def up_add(i):
        core_add(g1, 4 + i, i)
        if i < 2:
            free()

    def norm_back():
        normed = n1[...]
        gradient = res[...]
        residual_grad = normalize_back(gradient, normed, r1[...], gain[0:1])
        res[...] = residual_grad
        bgrad[...] = residual_grad.astype(bf16)
        vec[0:1, :] = row_sum(bgrad[...].astype(f32))
        vec[2:3, :] = row_sum(gradient * normed)
        vec[4:5, :] = row_sum(gradient)

    def heads_back(i):
        context_grad = dot(bgrad[...], W[0, i, 1, 1].reshape(192, 768), 1, 1).astype(bf16)
        for j in range(3):
            q = qkv[i, :, j * 64 : (j + 1) * 64]
            k = qkv[i, :, 192 + j * 64 : 192 + (j + 1) * 64]
            v = qkv[i, :, 384 + j * 64 : 384 + (j + 1) * 64]
            dc = context_grad[:, j * 64 : (j + 1) * 64]
            scores = jnp.where(visible, dot(k, q, 1, 1) * scaling, -1e30)
            attend = jnp.exp(scores - lse[i, j : j + 1, :])
            prob_grad = dot(v, dc, 1, 1)
            inner = jnp.sum(prob_grad * attend, axis=0, keepdims=True)
            score_grad = (attend * (prob_grad - inner)).astype(bf16)
            value_grad = dot(attend.astype(bf16), dc, 1, 0)
            key_grad = dot(score_grad, q, 1, 0) * scaling
            query_grad = dot(score_grad, k, 0, 0) * scaling
            qkv[i, :, j * 64 : (j + 1) * 64] = query_grad.astype(bf16)
            qkv[i, :, 192 + j * 64 : 192 + (j + 1) * 64] = key_grad.astype(bf16)
            qkv[i, :, 384 + j * 64 : 384 + (j + 1) * 64] = value_grad.astype(bf16)
        grads = qkv[i]
        res[...] += dot(grads, W[0, i].reshape(768, 768)[0:576], 1, 0)
        vec[pl.ds(10 + i, 1), 0:576] = row_sum(grads.astype(f32))

    def in_grad(i):
        made = dot(qkv[i], resb[...], 0, 0).astype(bf16)
        g0[i, 0] = made[0:384].reshape(2, 2, 2, R, 768)
        g0[i, 1, 0] = made[384:576].reshape(2, 2, R, 768)
        g0[i, 1, 1] = dot(ctx[i], bgrad[...], 0, 0).astype(bf16).reshape(2, 2, R, 768)
        wait_free()
        core_send(g0, 8 + i, i)

    def in_add(i):
        core_add(g0, 8 + i, i)

    def table_grad(h):
        if h == 0:
            hid[...] = res[...].astype(bf16)
        hot = one_hot(boxes[h : h + 1], boxes[h + 2 : h + 3], levels)
        made = dot(hot, hid[...], 1, 0).astype(bf16)
        act[4 * h : 4 * h + 4] = made.reshape(4, 2, 2, 2, 2, RT, 768)
        if h == 0:
            act[3, 1, 1, 1, 1] = vec[...].astype(bf16)
        remote(tables[h].at[:, 1 - c], core_land_t.at[h], ks.at[12 + h], kr.at[12 + h], C).start()

    def table_add(h):
        wait_recv(core_land_t.at[h], kr.at[12 + h])
        tables[h][:, c] = tables[h][:, c] + core_land_t[h]
        if h == 0:
            for k in range(4):
                zf_send(*zft, k)

    F = [g0.at[t, c, y, x], g1.at[t, c, y, x], G2.at[t, c, y, x]]
    F += [ref.at[t, c, y, x] for ref in tables]
    back = [G.at[0], G.at[1], G.at[2], GT.at[0, t], GT.at[1, t]]
    item = [9, 10, 11, 12, 16]
    kept = [pltpu.make_async_copy(F[b], back[b].at[c, y, x], loc.at[10 + b]) for b in range(5)]

    def ag_own(b):
        across(F[b], extra_t if b >= 3 else extra, b)
        kept[b].start()
        xy_own(F[b], back[b], item[b])

    def ag_relay(b):
        xy_relay(back[b], item[b])

    def ag_finish(b):
        kept[b].wait()
        xy_finish(back[b], item[b])

    def table_out(h):
        ag_own(3 + h)
        for j in range(1, 4):
            send, recv = zs.at[5 + h, j - 1], zr.at[5 + h, j - 1]
            remote(F[3 + h], GT.at[h, t, c, y, x], send, recv, (d, (t + j) % 4)).start()

    def table_in(h, j):
        ref = GT.at[h, (t + 4 - j) % 4]
        wait_recv(ref.at[c, y, x], zr.at[5 + h, j - 1])
        xy_own(ref.at[c, y, x], ref, 12 + 4 * h + j)

    def table_relay(h, j):
        xy_relay(GT.at[h, (t + 4 - j) % 4], 12 + 4 * h + j)

    def table_finish(h, j):
        if j == 0:
            kept[3 + h].wait()
        xy_finish(GT.at[h, (t + 4 - j) % 4], 12 + 4 * h + j)

    def first_grads(i, _):
        down_grad(i)
        events(i, [], [], [(down_add, 0)], [(down_add, 1), (xy1_send, *b2_low)])
        return 0

    def second_grads(i, _):
        @pl.when(i < 4)
        def _():
            @pl.when(i == 3)
            def _():
                out_copy.wait()

            down_act(i)

        events(
            i,
            [(down_add, 2)],
            [(down_add, 3), (xy1_send, *b2_high), (drain_late,)],
            [],
            [(xy1_add, *b2_low), (up_add, 0)],
            [(up_add, 1), (xy1_send, *b1_low)],
        )

        @pl.when(i >= 1)
        def _():
            up_grad(i - 1)

        return 0

    def third_grads(i, _):
        up_act(i)
        events(
            i,
            [(xy1_add, *b2_high), (up_add, 2)],
            [(up_add, 3), (xy2_add, *b2_low)],
            [],
            [(xy1_send, *b1_high)],
        )
        return 0

    def fourth_grads(i, _):
        heads_back(i)
        events(
            i,
            [(xy1_add, *b1_low), (xy2_add, *b2_high), (z_send, *z2)],
            [(in_add, 0)],
            [(xy2_add, *b1_high), (zk_send, *z1, 2), (zk_send, *z1, 3), (zf_sum, *zf2), (xy1_send, *f2)],
        )

        @pl.when(i < 3)
        def _():
            in_grad(i)

        events(
            i,
            [],
            [
                (xy1_add, *b1_high),
                (xy2_add, *b1_low),
                (zk_send, *z1, 0),
                (zk_send, *z1, 1),
                (in_add, 1),
                (xy1_send, *b0_low),
            ],
        )
        return 0

    lax.fori_loop(0, 4, first_grads, 0)
    lax.fori_loop(0, 5, second_grads, 0)
    lax.fori_loop(0, 4, third_grads, 0)
    norm_back()
    lax.fori_loop(0, 4, fourth_grads, 0)
    hidden_copy = pltpu.make_async_copy(res, grad_hidden, loc.at[9])
    hidden_copy.start()
    xy1_add(*b0_low)
    xy1_add(*f2)
    in_add(2)
    table_grad(0)
    table_grad(1)
    table_add(0)
    in_grad(3)
    table_add(1)
    xy1_send(*table1)
    xy2_add(*b0_low)
    xy2_add(*f2)
    in_add(3)
    z_sum(*z2)
    xy1_add(*table1)
    xy1_send(*b0_q2)
    z_sum(*z1)
    xy2_add(*table1)
    z_send(*zt1)
    xy1_send(*b0_q3)
    ag_own(2)
    xy1_add(*b0_q2)
    ag_own(1)
    zf_sum(*zft)
    xy1_send(*ft)
    z_sum(*zt1)
    table_out(1)
    ag_relay(2)
    xy1_add(*ft)
    xy1_add(*b0_q3)
    xy2_add(*b0_q2)
    xy2_add(*ft)
    table_out(0)
    for k in range(3):
        zk_send(*z0, k)
    ag_relay(1)
    xy2_add(*b0_q3)
    zk_send(*z0, 3)
    table_in(1, 1)
    table_relay(1, 0)
    table_in(1, 2)
    table_in(1, 3)
    table_in(0, 1)
    table_relay(0, 0)
    table_in(0, 2)
    table_in(0, 3)
    ag_finish(2)
    table_relay(1, 1)
    table_relay(1, 2)
    table_relay(1, 3)
    ag_finish(1)
    table_relay(0, 1)
    table_relay(0, 2)
    table_relay(0, 3)
    table_finish(1, 0)
    table_finish(1, 1)
    z_sum(*z0)
    ag_own(0)
    table_finish(1, 2)
    table_finish(1, 3)
    table_finish(0, 0)
    table_finish(0, 1)
    table_finish(0, 2)
    table_finish(0, 3)
    ag_relay(0)
    ag_finish(0)

    hidden_copy.wait()
    for j in range(3):
        wait_send(bias.at[0], bs.at[j])
    for n in range(12):
        wait_send(core_land.at[0], ks.at[n])
    for h in range(2):
        wait_send(core_land_t.at[h], ks.at[12 + h])
    for group in (b2_low, b2_high, b1_low, b1_high, b0_low, b0_q2, b0_q3, table1, f2, ft):
        xy_rs_drain(*group[3:])
    for group in (z0, z1, z2, zt1):
        z_drain_sum(*group[2:])
    z_drain_sum(zlf, 7)
    z_drain_sum(zlft, 3)
    z_drain_sum(zlt, 5)
    z_drain_sum(zlt, 6)
    for b in range(3):
        xy_drain(back[b], 9 + b)
        xy_done(back[b], 9 + b)
    for h in range(2):
        for j in range(4):
            ref = GT.at[h, (t + 4 - j) % 4]
            xy_drain(ref, 12 + 4 * h + j)
            xy_done(ref, 12 + 4 * h + j)


def finish(
    G,
    GT,
    table_x,
    table_y,
    in_w,
    out_w,
    up_w,
    down_w,
    in_b,
    out_b,
    up_b,
    down_b,
    gain,
    nbias,
    wide_w,
    wide_t,
    full_w,
    full_t,
    sem_in,
    sem_out,
):
    t = lax.axis_index("tensor")
    places = [in_w.at[0], in_w.at[1], in_w.at[2], out_w]
    places += [ref.at[pl.ds(192 * i, 192)] for ref in (up_w, down_w) for i in range(4)]
    tables = [ref.at[pl.ds(256 * i, 256)] for ref in (table_x, table_y) for i in range(4)]
    ins = [pltpu.make_async_copy(GT.at[i], wide_t.at[i], sem_in.at[12 + i]) for i in range(8)]
    ins = [pltpu.make_async_copy(G.at[i], wide_w.at[i], sem_in.at[i]) for i in range(12)] + ins
    outs = [pltpu.make_async_copy(full_w.at[i], places[i], sem_out.at[i]) for i in range(12)]
    outs += [pltpu.make_async_copy(full_t.at[i], tables[i], sem_out.at[12 + i]) for i in range(8)]
    for copy in ins:
        copy.start()
    for i in range(12):
        ins[i].wait()
        full_w[i] = wide_w[i].astype(f32)
        outs[i].start()
    for i in range(8):
        ins[12 + i].wait()
        full_t[i] = wide_t[i].astype(f32)
        if i == 3:
            small = wide_t[3, 240:256].astype(f32)
            full_t[3, 240:256, :] = jnp.zeros((16, 768), f32)
            gain[...] = small[2:4]
            nbias[...] = small[4:6]
            out_b[...] = small[0]
            down_b[...] = small[1]
            level = lax.broadcasted_iota(jnp.int32, (16, 1), 0)
            up_b[...] = jnp.sum(jnp.where(level == 6 + t, small, 0.0), axis=0)
            row = jnp.sum(jnp.where(level == 10 + t, small, 0.0), axis=0, keepdims=True)
            in_b[0:1, :] = row[:, 0:192]
            in_b[1:2, :] = row[:, 384:576]
        outs[12 + i].start()
    for copy in outs:
        copy.wait()


def on_device(
    dp,
    hidden,
    page_boxes,
    lengths,
    table_x,
    table_y,
    in_weight,
    in_bias,
    out_weight,
    out_bias,
    up_weight,
    up_bias,
    down_weight,
    down_bias,
    norm_gain,
    norm_bias,
    cotangent,
):
    blocks = (2, 2, 2, 2)
    vmem = pl.BlockSpec(memory_space=pltpu.VMEM)
    anywhere = pl.BlockSpec(memory_space=pl.ANY)
    dma = pltpu.SemaphoreType.DMA
    count = max(1, (dp // 8).bit_length() - 1)
    V = pltpu.VMEM

    def lands(quarters, rows):
        first, second = V((quarters, 2, rows, 768), bf16), V((quarters, rows, 768), bf16)
        return [first, first, second, second]

    scratch = [
        V((3, 4, *blocks, R, 768), bf16),
        V((4, *blocks, R, 768), bf16),
        V((2048, 768), bf16),
        V((8, *blocks, RT, 768), bf16),
        V((4, 512, 768), bf16),
        V((4, 512, 576), bf16),
        V((4, 512, 192), bf16),
        V((4, 8, 512), f32),
        V((512, 768), bf16),
        V((512, 768), bf16),
        V((512, 768), bf16),
        V((512, 768), bf16),
        V((512, 768), f32),
        V((512, 768), f32),
        V((512, 768), f32),
        V((512, 1), f32),
        V((4, 8, 768), f32),
        V((16, 768), f32),
        V((6, 2, 2, 2, R, 768), bf16),
        V((2, 4, 2, 2, 2, RT, 768), bf16),
        lands(4, R),
        lands(4, R),
        lands(4, XR),
        lands(4, RT),
        lands(1, FR),
        lands(1, RT),
        V((3, 2, R, 768), bf16),
        V((3, 2, R, 768), bf16),
        V((3, 2, XR, 768), bf16),
        V((3, 2, RT, 768), bf16),
        V((3, 2, 2, 2, FR, 768), bf16),
        V((3, 2, 2, 2, RT, 768), bf16),
        V((count, 2, R, 768) if dp > 8 else (8, 128), bf16),
        V((count, 2, RT, 768) if dp > 8 else (8, 128), bf16),
        dma((15,)),
        dma((3,)),
        dma((3,)),
        dma((3, 5, 2)),
        dma((3, 4, 2)),
        dma((2, 5)),
        dma((2, 4)),
        dma((20, 6)),
        dma((20, 6)),
        dma((20,)),
        dma((20,)),
        dma((14,)),
        dma((14,)),
        pltpu.SemaphoreType.REGULAR,
        dma((10, 4)),
        dma((10, 4)),
        dma((8, 3)),
        dma((8, 3)),
        dma((5, count)),
        dma((5, count)),
    ]
    shape = jax.ShapeDtypeStruct
    made_out, made_hidden, G, GT = pl.pallas_call(
        partial(kernel, dp),
        out_shape=(
            shape((512, 768), bf16),
            shape((512, 768), f32),
            shape((3, *blocks, R, 768), bf16),
            shape((2, 4, *blocks, RT, 768), bf16),
        ),
        in_specs=[
            anywhere,
            vmem,
            pl.BlockSpec(memory_space=pltpu.SMEM),
            anywhere,
            anywhere,
            anywhere,
            vmem,
            anywhere,
            vmem,
            anywhere,
            vmem,
            anywhere,
            vmem,
            vmem,
            vmem,
            anywhere,
        ],
        out_specs=(anywhere,) * 4,
        scratch_shapes=scratch,
        compiler_params=pltpu.CompilerParams(
            collective_id=0, has_side_effects=True, vmem_limit_bytes=61 * 2**20
        ),
    )(
        hidden,
        page_boxes.T,
        lengths,
        table_x,
        table_y,
        in_weight.transpose(0, 2, 1).reshape(3, 2, 2, R, 768),
        in_bias,
        out_weight.reshape(2, 2, R, 768),
        out_bias,
        up_weight.reshape(*blocks, R, 768),
        up_bias,
        down_weight.reshape(*blocks, R, 768),
        down_bias,
        norm_gain,
        norm_bias,
        cotangent,
    )
    outs = pl.pallas_call(
        finish,
        out_shape=(
            shape((1024, 768), f32),
            shape((1024, 768), f32),
            shape((3, 192, 768), f32),
            shape((192, 768), f32),
            shape((768, 768), f32),
            shape((768, 768), f32),
            shape((2, 192), f32),
            shape((768,), f32),
            shape((768,), f32),
            shape((768,), f32),
            shape((2, 768), f32),
            shape((2, 768), f32),
        ),
        in_specs=[pl.BlockSpec(memory_space=pltpu.HBM)] * 2,
        out_specs=(anywhere,) * 6 + (vmem,) * 6,
        scratch_shapes=[
            V((12, 192, 768), bf16),
            V((8, 256, 768), bf16),
            V((12, 192, 768), f32),
            V((8, 256, 768), f32),
            dma((20,)),
            dma((20,)),
        ],
        compiler_params=pltpu.CompilerParams(vmem_limit_bytes=62 * 2**20),
    )(G.reshape(12, 192, 768), GT.reshape(8, 256, 768))
    out, hidden_grad, outs = lax.optimization_barrier((made_out, made_hidden, outs))
    tx, ty, in_w, out_w, up_w, down_w, in_b, out_b, up_b, down_b, gains, biases = outs
    in_w = in_w.transpose(0, 2, 1)
    return out, hidden_grad, tx, ty, in_w, in_b, out_w, out_b, up_w, up_b, down_w, down_b, gains, biases


def solution(mesh):
    both = ("dp", "tensor")
    in_specs = (
        P(both, None),
        P(both, None),
        P("dp"),
        P(),
        P(),
        P(None, None, "tensor"),
        P(None, "tensor"),
        P("tensor", None),
        P(),
        P(None, "tensor"),
        P("tensor"),
        P("tensor", None),
        P(),
        P(),
        P(),
        P(both, None),
    )
    out_specs = (
        P(both, None),
        P(both, None),
        P(),
        P(),
        P(None, None, "tensor"),
        P(None, "tensor"),
        P("tensor", None),
        P(),
        P(None, "tensor"),
        P("tensor"),
        P("tensor", None),
        P(),
        P(),
        P(),
    )
    return jax.shard_map(
        partial(on_device, mesh.shape["dp"]),
        mesh=mesh,
        in_specs=in_specs,
        out_specs=out_specs,
        check_vma=False,
    )
```

profile of v0, /device:TPU:0, one launch (start us, length us, event | category | flops | bytes accessed | tf_op | source)
XLA Modules:
  0.0 178.9 jit_solution(12755895224515530766)
XLA Ops:
  0.7 167.8 %shard_map.263 = (bf16[512,768]{1,0:T(8,128)(2,1)}, f32[512,768]{1,0:T(8,128)}, bf16[3,2,2,2,2,48,768]{6,5,4,3,2,1,0:T(8,128)(2,1)}, bf16[2,4,2,2,2,2,16,768]{7,6,5,4,3,2,1,0:T(8,128)(2,1)}) custom-call(bf16[512,768]{1,0:T(8,128)(2,1)} %hidden.1, s32[4,512]{1,0:T(4,128)} %bitcast.16, s32[4]{0:T(128)} %lengths.1, bf16[1024,768]{1,0:T(8,128)(2,1)} %tables_x.1, ...), custom_call_target="tpu_custom_call" | custom-call | tf_op jit(solution)/shard_map/pallas_call | solution.py:1019
  168.4 0.0 copy-start.1
  168.4 7.6 %shard_map.264 = (f32[1024,768]{1,0:T(8,128)}, f32[1024,768]{1,0:T(8,128)}, f32[3,192,768]{2,1,0:T(8,128)}, f32[192,768]{1,0:T(8,128)}, f32[768,768]{1,0:T(8,128...) custom-call(bf16[12,192,768]{2,1,0:T(8,128)(2,1)} %bitcast.10, ...), custom_call_target="tpu_custom_call" | custom-call | tf_op jit(solution)/shard_map/pallas_call | solution.py:1068
  176.0 0.0 copy-start
  176.0 0.0 copy-done.1
  176.0 0.9 copy.32
  176.9 0.8 copy-done
  177.7 1.1 copy.33
Async XLA Ops:
  168.4 7.6 %copy-start.1 = (bf16[512,768]{1,0:T(8,128)(2,1)S(1)}, bf16[512,768]{1,0:T(8,128)(2,1)}, u32[]{:S(2)}) copy-start(bf16[512,768]{1,0:T(8,128)(2,1)} %get-tuple-element.88) | copy-start | bytes 2359300
  176.0 1.7 copy-start
where the time goes:
time: 179 us
  Pallas kernels  175 us (98%)
  local copies, waits for them, and re-layouts  2.82 us (2%)
    pallas_call x1, Pallas kernels, on_device(): pl.pallas_call(partial(kernel, dp), out_shape=(shape((512, 768), bf16), s...  168 us
    pallas_call x1, Pallas kernels, on_device(): pl.pallas_call(finish, out_shape=(shape((1024, 768), f32), shape((1024, 7...  7.58 us

commit v1 on v0

--- a/solution.py
+++ b/solution.py
@@ -708,6 +708,44 @@
             kept[3 + h].wait()
         xy_finish(GT.at[h, (t + 4 - j) % 4], 12 + 4 * h + j)
 
+    def drain_first():
+        for j in range(3):
+            wait_send(bias.at[0], bs.at[j])
+        for n in range(12):
+            wait_send(core_land.at[0], ks.at[n])
+        for h in range(2):
+            wait_send(core_land_t.at[h], ks.at[12 + h])
+        for group in (b2_low, b2_high, b1_low, b1_high, b0_low, f2, table1):
+            xy_rs_drain(*group[3:])
+        for group in (z1, z2):
+            z_drain_sum(*group[2:])
+        z_drain_sum(zlf, 7)
+
+    def drain_second():
+        hidden_copy.wait()
+        for group in (b0_q2, b0_q3, ft):
+            xy_rs_drain(*group[3:])
+        z_drain_sum(zlt, 4)
+        z_drain_sum(zlft, 3)
+
+    def drain_third():
+        z_drain_sum(zlt, 5)
+        z_drain_sum(zlt, 6)
+        z_drain_sum(*z0[2:])
+        for b in (1, 2):
+            xy_drain(back[b], 9 + b)
+            xy_done(back[b], 9 + b)
+
+    def drain_tables(h):
+        for j in range(4):
+            xy_drain(GT.at[h, (t + 4 - j) % 4], 12 + 4 * h + j)
+            xy_done(GT.at[h, (t + 4 - j) % 4], 12 + 4 * h + j)
+
+    def drain_back():
+        drain_tables(0)
+        xy_drain(back[0], 9)
+        xy_done(back[0], 9)
+
     def first_grads(i, _):
         down_grad(i)
         events(i, [], [], [(down_add, 0)], [(down_add, 1), (xy1_send, *b2_low)])
@@ -803,13 +841,14 @@
     xy1_send(*b0_q3)
     ag_own(2)
     xy1_add(*b0_q2)
-    ag_own(1)
     zf_sum(*zft)
     xy1_send(*ft)
     z_sum(*zt1)
     table_out(1)
     ag_relay(2)
+    drain_first()
     xy1_add(*ft)
+    ag_own(1)
     xy1_add(*b0_q3)
     xy2_add(*b0_q2)
     xy2_add(*ft)
@@ -828,6 +867,7 @@
     table_in(0, 2)
     table_in(0, 3)
     ag_finish(2)
+    drain_second()
     table_relay(1, 1)
     table_relay(1, 2)
     table_relay(1, 3)
@@ -846,36 +886,20 @@
     table_finish(0, 2)
     table_finish(0, 3)
     ag_relay(0)
+    drain_third()
+    drain_tables(1)
     ag_finish(0)
 
-    hidden_copy.wait()
-    for j in range(3):
-        wait_send(bias.at[0], bs.at[j])
-    for n in range(12):
-        wait_send(core_land.at[0], ks.at[n])
-    for h in range(2):
-        wait_send(core_land_t.at[h], ks.at[12 + h])
-    for group in (b2_low, b2_high, b1_low, b1_high, b0_low, b0_q2, b0_q3, table1, f2, ft):
-        xy_rs_drain(*group[3:])
-    for group in (z0, z1, z2, zt1):
-        z_drain_sum(*group[2:])
-    z_drain_sum(zlf, 7)
-    z_drain_sum(zlft, 3)
-    z_drain_sum(zlt, 5)
-    z_drain_sum(zlt, 6)
-    for b in range(3):
-        xy_drain(back[b], 9 + b)
-        xy_done(back[b], 9 + b)
-    for h in range(2):
-        for j in range(4):
-            ref = GT.at[h, (t + 4 - j) % 4]
-            xy_drain(ref, 12 + 4 * h + j)
-            xy_done(ref, 12 + 4 * h + j)
+    drain_back()
 
 
 def finish(
     G,
     GT,
+    made_out,
+    made_hidden,
+    layer_out,
+    grad_hidden,
     table_x,
     table_y,
     in_w,
@@ -892,6 +916,8 @@
     wide_t,
     full_w,
     full_t,
+    held_out,
+    held_hidden,
     sem_in,
     sem_out,
 ):
@@ -903,6 +929,14 @@
     ins = [pltpu.make_async_copy(G.at[i], wide_w.at[i], sem_in.at[i]) for i in range(12)] + ins
     outs = [pltpu.make_async_copy(full_w.at[i], places[i], sem_out.at[i]) for i in range(12)]
     outs += [pltpu.make_async_copy(full_t.at[i], tables[i], sem_out.at[12 + i]) for i in range(8)]
+    ins += [
+        pltpu.make_async_copy(made_hidden, held_hidden, sem_in.at[20]),
+        pltpu.make_async_copy(made_out, held_out, sem_in.at[21]),
+    ]
+    outs += [
+        pltpu.make_async_copy(held_hidden, grad_hidden, sem_out.at[20]),
+        pltpu.make_async_copy(held_out, layer_out, sem_out.at[21]),
+    ]
     for copy in ins:
         copy.start()
     for i in range(12):
@@ -925,6 +959,9 @@
             in_b[0:1, :] = row[:, 0:192]
             in_b[1:2, :] = row[:, 384:576]
         outs[12 + i].start()
+    for i in (20, 21):
+        ins[i].wait()
+        outs[i].start()
     for copy in outs:
         copy.wait()
 
@@ -1068,6 +1105,8 @@
     outs = pl.pallas_call(
         finish,
         out_shape=(
+            shape((512, 768), bf16),
+            shape((512, 768), f32),
             shape((1024, 768), f32),
             shape((1024, 768), f32),
             shape((3, 192, 768), f32),
@@ -1081,20 +1120,21 @@
             shape((2, 768), f32),
             shape((2, 768), f32),
         ),
-        in_specs=[pl.BlockSpec(memory_space=pltpu.HBM)] * 2,
-        out_specs=(anywhere,) * 6 + (vmem,) * 6,
+        in_specs=[pl.BlockSpec(memory_space=pltpu.HBM)] * 4,
+        out_specs=(anywhere,) * 8 + (vmem,) * 6,
         scratch_shapes=[
             V((12, 192, 768), bf16),
             V((8, 256, 768), bf16),
             V((12, 192, 768), f32),
             V((8, 256, 768), f32),
-            dma((20,)),
-            dma((20,)),
+            V((512, 768), bf16),
+            V((512, 768), f32),
+            dma((22,)),
+            dma((22,)),
         ],
         compiler_params=pltpu.CompilerParams(vmem_limit_bytes=62 * 2**20),
-    )(G.reshape(12, 192, 768), GT.reshape(8, 256, 768))
-    out, hidden_grad, outs = lax.optimization_barrier((made_out, made_hidden, outs))
-    tx, ty, in_w, out_w, up_w, down_w, in_b, out_b, up_b, down_b, gains, biases = outs
+    )(G.reshape(12, 192, 768), GT.reshape(8, 256, 768), made_out, made_hidden)
+    out, hidden_grad, tx, ty, in_w, out_w, up_w, down_w, in_b, out_b, up_b, down_b, gains, biases = outs
     in_w = in_w.transpose(0, 2, 1)
     return out, hidden_grad, tx, ty, in_w, in_b, out_w, out_b, up_w, up_b, down_w, down_b, gains, biases
 

time: 179 us -> 178 us (level)
  local copies, waits for them, and re-layouts: 2.82 us -> 0 us
  Pallas kernels: 175 us -> 177 us
    unnamed x6 -> x0, local copies, waits for them, and re-layouts: 2.82 us -> none
    pallas_call x1, Pallas kernels: 7.58 us -> 9.42 us  [on_device(): pl.pallas_call(finish, out_shape=(shape((512, 768), bf16), shape((512, 76...]
where the time goes in v1:
time: 178 us
  Pallas kernels  177 us (99%)
    pallas_call x1, Pallas kernels, on_device(): pl.pallas_call(partial(kernel, dp), out_shape=(shape((512, 768), bf16), s...  167 us
    pallas_call x1, Pallas kernels, on_device(): pl.pallas_call(finish, out_shape=(shape((512, 768), bf16), shape((512, 76...  9.42 us

profile of v1, /device:TPU:0, one launch (start us, length us, event | category | flops | bytes accessed | tf_op | source)
XLA Modules:
  0.0 177.7 jit_solution(9898726085080753690)
XLA Ops:
  0.7 167.4 %shard_map.263 = (bf16[512,768]{1,0:T(8,128)(2,1)}, f32[512,768]{1,0:T(8,128)}, bf16[3,2,2,2,2,48,768]{6,5,4,3,2,1,0:T(8,128)(2,1)}, bf16[2,4,2,2,2,2,16,768]{7,6,5,4,3,2,1,0:T(8,128)(2,1)}) custom-call(bf16[512,768]{1,0:T(8,128)(2,1)} %hidden.1, s32[4,512]{1,0:T(4,128)} %bitcast.16, s32[4]{0:T(128)} %lengths.1, bf16[1024,768]{1,0:T(8,128)(2,1)} %tables_x.1, ...), custom_call_target="tpu_custom_call" | custom-call | tf_op jit(solution)/shard_map/pallas_call | solution.py:1056
  168.1 9.4 %shard_map.264 = (bf16[512,768]{1,0:T(8,128)(2,1)}, f32[512,768]{1,0:T(8,128)}, f32[1024,768]{1,0:T(8,128)}, f32[1024,768]{1,0:T(8,128)}, f32[3,192,768]{2,1,0:T...) custom-call(bf16[12,192,768]{2,1,0:T(8,128)(2,1)} %bitcast.10, ...), custom_call_target="tpu_custom_call" | custom-call | tf_op jit(solution)/shard_map/pallas_call | solution.py:1105

commit v2 on v1

--- a/solution.py
+++ b/solution.py
@@ -204,16 +204,16 @@
         a, b = src.at[0], src.at[1]
         da, db = dst.at[c, y, x, 0], dst.at[c, y, x, 1]
         remote(a, da, xs.at[i, 0], xr.at[i, 0], X).start()
-        remote(b, db, xs.at[i, 2], xr.at[i, 2], Y).start()
-        remote(a, da, xs.at[i, 1], xr.at[i, 1], Y).start()
-        remote(b, db, xs.at[i, 3], xr.at[i, 3], X).start()
+        remote(b, db, xs.at[i, 1], xr.at[i, 2], Y).start()
+        remote(a, da, xs.at[i, 0], xr.at[i, 1], Y).start()
+        remote(b, db, xs.at[i, 1], xr.at[i, 3], X).start()
 
     def xy_relay(ref, i, ra=slice(None), rb=slice(None)):
         a, b = ref.at[c, y, 1 - x, 0, ra], ref.at[c, 1 - y, x, 1, rb]
         wait_recv(a, xr.at[i, 0])
-        remote(a, a, xs.at[i, 4], xr.at[i, 4], Y).start()
+        remote(a, a, xs.at[i, 0], xr.at[i, 4], Y).start()
         wait_recv(b, xr.at[i, 2])
-        remote(b, b, xs.at[i, 5], xr.at[i, 5], X).start()
+        remote(b, b, xs.at[i, 1], xr.at[i, 5], X).start()
 
     def xy_finish(ref, i, ra=slice(None), rb=slice(None)):
         wait_recv(ref.at[c, 1 - y, x, 0, ra], xr.at[i, 1])
@@ -225,9 +225,9 @@
     def xy_done(ref, i):
         wait_recv(ref.at[1 - c], cr.at[i])
 
-    def xy_drain(ref, i, ra=slice(None), rb=slice(None)):
-        for k in range(6):
-            wait_send(ref.at[c, 0, 0, 0, ra if k in (0, 1, 4) else rb], xs.at[i, k])
+    def xy_drain(ref, i, rows_a, rows_b):
+        for h, count in enumerate((rows_a, rows_b)):
+            wait_send(pre.at[pl.ds(0, 3 * count)], xs.at[i, h])
         wait_send(ref.at[c], cs.at[i])
 
     def rows_of(b, h):
@@ -268,7 +268,7 @@
             ref = W.at[b, tp, c, y, x, h, rows_of(b, h)]
             z_arrive(ref, tp, gzs.at[b, 2 + j, h], gzr.at[b, tp, h])
             for dev, k in ((X, 0), (Y, 1)) if h == 0 else ((Y, 2), (X, 3)):
-                remote(ref, ref, xs.at[i, k], xr.at[i, k], dev).start()
+                remote(ref, ref, xs.at[i, h], xr.at[i, k], dev).start()
 
     def e2(i):
         xy_relay(W.at[i // 3, other(i % 3)], i, *both(i // 3))
@@ -374,7 +374,7 @@
 
     def drain_items(b):
         def one(j, _):
-            xy_drain(W.at[0, 0], 3 * b + j, *both(b))
+            xy_drain(W.at[0, 0], 3 * b + j, *(r.size for r in both(b)))
             return 0
 
         lax.fori_loop(0, 3, one, 0)
@@ -733,17 +733,17 @@
         z_drain_sum(zlt, 6)
         z_drain_sum(*z0[2:])
         for b in (1, 2):
-            xy_drain(back[b], 9 + b)
+            xy_drain(back[b], 9 + b, R, R)
             xy_done(back[b], 9 + b)
 
     def drain_tables(h):
         for j in range(4):
-            xy_drain(GT.at[h, (t + 4 - j) % 4], 12 + 4 * h + j)
+            xy_drain(GT.at[h, (t + 4 - j) % 4], 12 + 4 * h + j, RT, RT)
             xy_done(GT.at[h, (t + 4 - j) % 4], 12 + 4 * h + j)
 
     def drain_back():
         drain_tables(0)
-        xy_drain(back[0], 9)
+        xy_drain(back[0], 9, R, R)
         xy_done(back[0], 9)
 
     def first_grads(i, _):
@@ -1038,7 +1038,7 @@
         dma((3, 4, 2)),
         dma((2, 5)),
         dma((2, 4)),
-        dma((20, 6)),
+        dma((20, 2)),
         dma((20, 6)),
         dma((20,)),
         dma((20,)),

time: 178 us -> 177 us (level)
  no operation moved by 1% of the time
where the time goes in v2:
time: 177 us
  Pallas kernels  176 us (99%)
    pallas_call x1, Pallas kernels, on_device(): pl.pallas_call(partial(kernel, dp), out_shape=(shape((512, 768), bf16), s...  167 us
    pallas_call x1, Pallas kernels, on_device(): pl.pallas_call(finish, out_shape=(shape((512, 768), bf16), shape((512, 76...  9.42 us

profile of v2, /device:TPU:0, one launch (start us, length us, event | category | flops | bytes accessed | tf_op | source)
XLA Modules:
  0.0 176.9 jit_solution(17699924289569635190)
XLA Ops:
  0.7 166.7 %shard_map.263 = (bf16[512,768]{1,0:T(8,128)(2,1)}, f32[512,768]{1,0:T(8,128)}, bf16[3,2,2,2,2,48,768]{6,5,4,3,2,1,0:T(8,128)(2,1)}, bf16[2,4,2,2,2,2,16,768]{7,6,5,4,3,2,1,0:T(8,128)(2,1)}) custom-call(bf16[512,768]{1,0:T(8,128)(2,1)} %hidden.1, s32[4,512]{1,0:T(4,128)} %bitcast.16, s32[4]{0:T(128)} %lengths.1, bf16[1024,768]{1,0:T(8,128)(2,1)} %tables_x.1, ...), custom_call_target="tpu_custom_call" | custom-call | tf_op jit(solution)/shard_map/pallas_call | solution.py:1056
  167.3 9.4 %shard_map.264 = (bf16[512,768]{1,0:T(8,128)(2,1)}, f32[512,768]{1,0:T(8,128)}, f32[1024,768]{1,0:T(8,128)}, f32[1024,768]{1,0:T(8,128)}, f32[3,192,768]{2,1,0:T...) custom-call(bf16[12,192,768]{2,1,0:T(8,128)(2,1)} %bitcast.10, ...), custom_call_target="tpu_custom_call" | custom-call | tf_op jit(solution)/shard_map/pallas_call | solution.py:1105

commit v3 on v2

--- a/solution.py
+++ b/solution.py
@@ -480,7 +480,7 @@
     vec[5:6, :] = row_sum(gradient)
 
     def core_send(ref, n, tp):
-        remote(ref.at[tp, 1 - c], core_land.at[n % 6], ks.at[n], kr.at[n], C).start()
+        remote(ref.at[tp, 1 - c], core_land.at[n % 6], ks.at[n // 4], kr.at[n], C).start()
 
     def core_add(ref, n, tp):
         wait_recv(core_land.at[n % 6], kr.at[n])
@@ -495,16 +495,16 @@
     def xy1_send(ref, part, rows, lands, lp, g):
         a = ref.at[part, c, :, 1 - x, 0, rows]
         b = ref.at[part, c, 1 - y, :, 1, rows]
-        remote(a, lands[0].at[lp], rs.at[g, 0], rr.at[g, 0], X).start()
-        remote(b, lands[1].at[lp], rs.at[g, 1], rr.at[g, 1], Y).start()
+        remote(a, lands[0].at[lp], rs.at[g], rr.at[g, 0], X).start()
+        remote(b, lands[1].at[lp], rs.at[g], rr.at[g, 1], Y).start()
 
     def xy1_add(ref, part, rows, lands, lp, g):
         wait_recv(lands[0].at[lp], rr.at[g, 0])
         ref[part, c, :, x, 0, rows] = ref[part, c, :, x, 0, rows] + lands[0][lp]
-        remote(ref.at[part, c, 1 - y, x, 0, rows], lands[3].at[lp], rs.at[g, 3], rr.at[g, 3], Y).start()
+        remote(ref.at[part, c, 1 - y, x, 0, rows], lands[3].at[lp], rs.at[g], rr.at[g, 3], Y).start()
         wait_recv(lands[1].at[lp], rr.at[g, 1])
         ref[part, c, y, :, 1, rows] = ref[part, c, y, :, 1, rows] + lands[1][lp]
-        remote(ref.at[part, c, y, 1 - x, 1, rows], lands[2].at[lp], rs.at[g, 2], rr.at[g, 2], X).start()
+        remote(ref.at[part, c, y, 1 - x, 1, rows], lands[2].at[lp], rs.at[g], rr.at[g, 2], X).start()
 
     def xy2_add(ref, part, rows, lands, lp, g):
         wait_recv(lands[3].at[lp], rr.at[g, 3])
@@ -513,19 +513,21 @@
         ref[part, c, y, x, 1, rows] = ref[part, c, y, x, 1, rows] + lands[2][lp]
 
     def xy_rs_drain(lands, lp, g):
-        for k in range(4):
-            wait_send(lands[k].at[lp], rs.at[g, k])
+        count = 1
+        for extent in lands[2].at[lp].shape[:-1]:
+            count *= extent
+        wait_send(pre.at[pl.ds(0, 6 * count)], rs.at[g])
 
     def z_send(ref, rows, land, g):
         for j in range(1, 4):
             k = (t + j) % 4
-            remote(ref.at[k, c, y, x, :, rows], land.at[j - 1], zs.at[g, j - 1], zr.at[g, j - 1], (d, k)).start()
+            remote(ref.at[k, c, y, x, :, rows], land.at[j - 1], zs.at[g], zr.at[g, j - 1], (d, k)).start()
 
     def zk_send(ref, rows, land, g, k):
         @pl.when(t != k)
         def _():
             slot = (k - t + 3) % 4
-            remote(ref.at[k, c, y, x, :, rows], land.at[slot], zs.at[g, slot], zr.at[g, slot], (d, k)).start()
+            remote(ref.at[k, c, y, x, :, rows], land.at[slot], zs.at[g], zr.at[g, slot], (d, k)).start()
 
     def z_sum(ref, rows, land, g):
         for j in range(3):
@@ -536,14 +538,13 @@
         ref[t, c, y, x, :, rows] = value.astype(bf16)
 
     def z_drain_sum(land, g):
-        for j in range(3):
-            wait_send(land.at[j], zs.at[g, j])
+        wait_send(land, zs.at[g])
 
     def zf_send(ref, rows, land, g, k):
         @pl.when(t != k)
         def _():
             slot = (k - t + 3) % 4
-            remote(ref.at[k, c, :, :, :, rows], land.at[slot], zs.at[g, slot], zr.at[g, slot], (d, k)).start()
+            remote(ref.at[k, c, :, :, :, rows], land.at[slot], zs.at[g], zr.at[g, slot], (d, k)).start()
 
     def zf_sum(ref, rows, land, g):
         for j in range(3):
@@ -662,7 +663,7 @@
         act[4 * h : 4 * h + 4] = made.reshape(4, 2, 2, 2, 2, RT, 768)
         if h == 0:
             act[3, 1, 1, 1, 1] = vec[...].astype(bf16)
-        remote(tables[h].at[:, 1 - c], core_land_t.at[h], ks.at[12 + h], kr.at[12 + h], C).start()
+        remote(tables[h].at[:, 1 - c], core_land_t.at[h], ks.at[3], kr.at[12 + h], C).start()
 
     def table_add(h):
         wait_recv(core_land_t.at[h], kr.at[12 + h])
@@ -692,7 +693,7 @@
     def table_out(h):
         ag_own(3 + h)
         for j in range(1, 4):
-            send, recv = zs.at[5 + h, j - 1], zr.at[5 + h, j - 1]
+            send, recv = zs.at[5 + h], zr.at[5 + h, j - 1]
             remote(F[3 + h], GT.at[h, t, c, y, x], send, recv, (d, (t + j) % 4)).start()
 
     def table_in(h, j):
@@ -711,10 +712,9 @@
     def drain_first():
         for j in range(3):
             wait_send(bias.at[0], bs.at[j])
-        for n in range(12):
-            wait_send(core_land.at[0], ks.at[n])
-        for h in range(2):
-            wait_send(core_land_t.at[h], ks.at[12 + h])
+        for n in range(3):
+            wait_send(pre.at[pl.ds(0, 1536)], ks.at[n])
+        wait_send(core_land_t, ks.at[3])
         for group in (b2_low, b2_high, b1_low, b1_high, b0_low, f2, table1):
             xy_rs_drain(*group[3:])
         for group in (z1, z2):
@@ -1042,12 +1042,12 @@
         dma((20, 6)),
         dma((20,)),
         dma((20,)),
-        dma((14,)),
+        dma((4,)),
         dma((14,)),
         pltpu.SemaphoreType.REGULAR,
+        dma((10,)),
         dma((10, 4)),
-        dma((10, 4)),
-        dma((8, 3)),
+        dma((8,)),
         dma((8, 3)),
         dma((5, count)),
         dma((5, count)),

time: 177 us -> 177 us (level)
  no operation moved by 1% of the time
where the time goes in v3:
time: 177 us; the launch traced here: 176 us
  Pallas kernels  176 us (99%)
    pallas_call x1, Pallas kernels, on_device(): pl.pallas_call(partial(kernel, dp), out_shape=(shape((512, 768), bf16), s...  166 us
    pallas_call x1, Pallas kernels, on_device(): pl.pallas_call(finish, out_shape=(shape((512, 768), bf16), shape((512, 76...  9.42 us

profile of v3, /device:TPU:0, one launch (start us, length us, event | category | flops | bytes accessed | tf_op | source)
XLA Modules:
  0.0 176.5 jit_solution(1475636284771343933)
XLA Ops:
  0.7 166.2 %shard_map.263 = (bf16[512,768]{1,0:T(8,128)(2,1)}, f32[512,768]{1,0:T(8,128)}, bf16[3,2,2,2,2,48,768]{6,5,4,3,2,1,0:T(8,128)(2,1)}, bf16[2,4,2,2,2,2,16,768]{7,6,5,4,3,2,1,0:T(8,128)(2,1)}) custom-call(bf16[512,768]{1,0:T(8,128)(2,1)} %hidden.1, s32[4,512]{1,0:T(4,128)} %bitcast.16, s32[4]{0:T(128)} %lengths.1, bf16[1024,768]{1,0:T(8,128)(2,1)} %tables_x.1, ...), custom_call_target="tpu_custom_call" | custom-call | tf_op jit(solution)/shard_map/pallas_call | solution.py:1056
  166.9 9.4 %shard_map.264 = (bf16[512,768]{1,0:T(8,128)(2,1)}, f32[512,768]{1,0:T(8,128)}, f32[1024,768]{1,0:T(8,128)}, f32[1024,768]{1,0:T(8,128)}, f32[3,192,768]{2,1,0:T...) custom-call(bf16[12,192,768]{2,1,0:T(8,128)(2,1)} %bitcast.10, ...), custom_call_target="tpu_custom_call" | custom-call | tf_op jit(solution)/shard_map/pallas_call | solution.py:1105
